TPU v7x, 32 devices: a whole 2x2x4 slice. The times are simulated.
32 devices in a mesh: row: 4 (over y, core), col: 8 (over z, x).
Axes of the slice: x: 2, y: 2, z: 4, core: 2. Of those that a mesh axis runs over, the one named last changes fastest.
Arguments:
- matrix: float32 [4, 4, 8, 256, 256], P(None, 'row', 'col'), as said below
- present: int32 [4, 4, 8], P(None, 'row', 'col'), may hold values from 0 to 1, as said below
- update: int32 [2, 4, 4, 8], P(None, None, 'row', 'col'), may hold values from 0 to 1, as said below
Outputs:
- factored: float32 [4, 4, 8, 256, 256], P(None, 'row', 'col')
Inputs may be any that keep to these rules, and one draw needn't show every extreme that they name: `present`: listed tiles lie on or below the diagonal (row >= column). Tiles (0, 0), (1, 0), (1, 1) and every diagonal tile (c, c) of the window, that is with c < 16 and c < 8, are listed; in column 1 every row i >= 1 whose tile in column 0 is listed is listed too. update[k, s, r, c] is 1 exactly where c > k and the tiles (i, c), (i, k) and (c, k) are all listed, with i = r + 4 s. `matrix`: unlisted tiles are zero. Tile (0, 0) is symmetric positive definite, and so is tile (1, 1) minus P0(1) P0(1)^T.
All inputs are finite; a program needn't handle non-finite values.
Results may differ from a plain program's by a relative error of at most 0.0001.
Values sent between devices are 32-bit elements; how exact they have to be, the bound alone decides.
A program may use at most 64 MiB of HBM per device.

v0:
```python
import functools

import jax
import jax.numpy as jnp
from jax import lax
from jax.experimental import pallas as pl
from jax.experimental.pallas import tpu as pltpu
from jax.sharding import PartitionSpec as P

MESH = pl.DeviceIdType.MESH
HI = lax.Precision.HIGHEST
NB = 64
GROUP = 4


def dot(a, b, contract):
    return lax.dot_general(
        a, b, (contract, ((), ())), precision=HI, preferred_element_type=jnp.float32
    )


def nn(a, b):
    return dot(a, b, ((1,), (0,)))


def nt(a, b):
    return dot(a, b, ((1,), (1,)))


def tn(a, b):
    return dot(a, b, ((0,), (0,)))


def invert_block(m):
    n = m.shape[0]
    done = []
    for k in range(0, n, GROUP):
        top = (k // 8) * 8
        off = k - top
        cols = [jnp.broadcast_to(m[:, k + t : k + t + 1], m.shape) for t in range(GROUP)]
        rows = [m[off + t : off + t + 1, :] for t in range(GROUP)]
        total = None
        for t in range(GROUP):
            pivot = cols[t][off + t : off + t + 1, :]
            inverse = 1.0 / pivot
            done.append(rows[t] * lax.rsqrt(pivot))
            scaled = rows[t] * inverse
            for u in range(t + 1, GROUP):
                entry = cols[u][off + t : off + t + 1, :]
                rows[u] = rows[u] - entry * scaled
                cols[u] = cols[u] - cols[t] * (entry * inverse)
            term = cols[t] * scaled
            total = term if total is None else total + term
        m = m - total
        if (k + GROUP) % 8 == 0:
            m = m[8:]
    return jnp.concatenate(done, axis=0)


def inverse_factor(work, block_inv):
    width = work.shape[0]
    blocks = width // NB

    def step(j, carry):
        rows = pl.ds(pl.multiple_of(j * NB, NB), NB)
        strip = work[rows, :]
        diag = strip[:, :NB]
        for b in range(1, blocks):
            diag = jnp.where(j == b, strip[:, b * NB : (b + 1) * NB], diag)
        eye = (
            lax.broadcasted_iota(jnp.int32, (NB, NB), 0)
            == lax.broadcasted_iota(jnp.int32, (NB, NB), 1)
        ).astype(jnp.float32)
        solved = invert_block(jnp.concatenate([diag, eye], axis=1))
        block = solved[:, NB:]
        strip = nn(block, strip)
        lane = lax.broadcasted_iota(jnp.int32, (NB, width), 1)
        upper = jnp.where(lane >= (j + 1) * NB, strip[:, :width], 0.0)
        work[...] = work[...] - tn(upper, strip)
        work[rows, :] = strip
        return carry

    lax.fori_loop(0, blocks, step, 0)


def kernel(
    n_row, n_col, m_ref, listed, update, o_ref, dbuf, far, lead, bc, work, wcol, acc, wfar, p0far,
    d_send, d_recv, far_send, far_recv, lead_send, lead_recv, bc_send, bc_recv,
):
    r = lax.axis_index("row")
    c = lax.axis_index("col")
    slots, width = m_ref.shape[0], m_ref.shape[-1]
    half = width // 2
    x = c % 2
    cross = c + 1 - 2 * x
    root = (r == 0) & (c == 0)
    lead_b = (r == 1) & (c == 1)
    far_row = c % n_row
    far_slot = jnp.minimum(c // n_row, slots - 1)

    def greet(row, col):
        pl.semaphore_signal(
            pltpu.get_barrier_semaphore(), inc=1, device_id=(row, col), device_id_type=MESH
        )

    barrier = pltpu.get_barrier_semaphore()
    for k in range(1, n_row):
        greet((r + k) % n_row, c)
    greet(r, cross)
    partners = n_row + (c >= 2).astype(jnp.int32) + (c + 2 < n_col).astype(jnp.int32)

    @pl.when(c >= 2)
    def _():
        greet(r, c - 2)

    @pl.when(c + 2 < n_col)
    def _():
        greet(r, c + 2)

    @pl.when(root)
    def _():
        greet(1, 1)

    @pl.when(lead_b)
    def _():
        greet(0, 0)

    @pl.when(c < 2)
    def _():
        dbuf[x] = m_ref[...]

    pl.semaphore_wait(barrier, partners + (root | lead_b).astype(jnp.int32))

    def lead_copy(q):
        return pltpu.make_async_remote_copy(
            m_ref.at[0], lead.at[q], lead_send.at[q], lead_recv.at[q],
            device_id=(0, 0), device_id_type=MESH,
        )

    lead_a = (r == 1) & (c == 0)

    @pl.when(lead_a)
    def _():
        lead_copy(0).start()

    @pl.when(lead_b)
    def _():
        lead_copy(1).start()

    def line_copy(s):
        return pltpu.make_async_remote_copy(
            dbuf.at[x, s], dbuf.at[x, s], d_send.at[0, s], d_recv.at[0, s],
            device_id=(r, c + 2), device_id_type=MESH,
        )

    def cross_copy(s, side):
        return pltpu.make_async_remote_copy(
            dbuf.at[side, s], dbuf.at[side, s], d_send.at[1, s], d_recv.at[1, s],
            device_id=(r, cross), device_id_type=MESH,
        )

    def line_need(col, s):
        return (col >= 2) & (col < n_col) & (r + n_row * s >= col - col % 2)

    def cross_need(col, s):
        return (col >= 1) & (r + n_row * s >= col)

    for s in range(slots):

        @pl.when(line_need(c, s))
        def _():
            line_copy(s).wait_recv()

        @pl.when(line_need(c + 2, s))
        def _():
            line_copy(s).start()

        @pl.when(cross_need(cross, s))
        def _():
            cross_copy(s, x).start()

    child = [
        ((r % 2 == 0) & (c == 0) & (r + 2 < n_row), (r + 2, c)),
        ((r % 2 == 0) & (c + 2 < n_col), (r, c + 2)),
        ((r % 2 == 0) & (c == 0), (r, c + 1)),
        ((r % 2 == 0) & (r + 1 < n_row), (r + 1, c)),
    ]

    def bc_copy(q, h, k):
        piece = bc.at[q, pl.ds(h * half, half)]
        return pltpu.make_async_remote_copy(
            piece, piece, bc_send.at[q, h, k], bc_recv.at[q, h],
            device_id=child[k][1], device_id_type=MESH,
        )

    def bc_start(q, h):
        for k in range(4):

            @pl.when(child[k][0])
            def _():
                bc_copy(q, h, k).start()

    def pass_on(q):
        for h in range(2):

            @pl.when(jnp.logical_not(root))
            def _():
                bc_copy(q, h, 0).wait_recv()
                bc_start(q, h)

    @pl.when(root)
    def _():
        eye = (
            lax.broadcasted_iota(jnp.int32, (width, width), 0)
            == lax.broadcasted_iota(jnp.int32, (width, width), 1)
        ).astype(jnp.float32)
        work[:, :width] = m_ref[0]
        work[:, width:] = eye
        inverse_factor(work, None)
        bc[0] = work[:, width:]
        bc_start(0, 0)
        bc_start(0, 1)
        lead_copy(0).wait_recv()
        lead_copy(1).wait_recv()
        p01 = nt(lead[0], work[:, width:])
        bc[1] = p01
        bc_start(1, 0)
        bc_start(1, 1)
        work[:, :width] = lead[1] - nt(p01, p01)
        work[:, width:] = eye
        inverse_factor(work, None)
        bc[2] = work[:, width:]
        bc_start(2, 0)
        bc_start(2, 1)

    for s in range(slots):

        @pl.when(cross_need(c, s))
        def _():
            cross_copy(s, 1 - x).wait_recv()

    def far_copy(k, q):
        return pltpu.make_async_remote_copy(
            dbuf.at[q, far_slot], far.at[q], far_send.at[k, q], far_recv.at[q],
            device_id=((r + k) % n_row, c), device_id_type=MESH,
        )

    @pl.when((c >= 1) & (r == far_row))
    def _():
        for k in range(1, n_row):
            for q in range(2):
                far_copy(k, q).start()
        for q in range(2):
            far[q] = dbuf[q, far_slot]

    @pl.when((c >= 1) & (r != far_row))
    def _():
        for q in range(2):
            far_copy(1, q).wait_recv()

    pass_on(0)
    pass_on(1)

    lower = lax.broadcasted_iota(jnp.int32, (width, width), 0) >= lax.broadcasted_iota(
        jnp.int32, (width, width), 1
    )

    @pl.when(c >= 2)
    def _():
        p0far[...] = nt(far[0], bc[0])
        wfar[...] = far[1] - nt(p0far[...], bc[1])

    for s in range(slots):
        inside = r + n_row * s >= c

        @pl.when(inside & (c == 0))
        def _():
            panel = nt(m_ref[s], bc[0])
            panel = jnp.where(lower | (r + n_row * s > 0), panel, 0.0)
            o_ref[s] = jnp.where(listed[s] > 0, panel, 0.0)

        @pl.when(inside & (c >= 1))
        def _():
            panel = nt(dbuf[0, s], bc[0])
            wcol[s] = dbuf[1, s] - nt(panel, bc[1])

            @pl.when(c >= 2)
            def _():
                product = nt(panel, p0far[...])
                acc[s] = m_ref[s] - jnp.where(update[s] > 0, product, 0.0)

    pass_on(2)

    @pl.when(c >= 2)
    def _():
        p1far = nt(wfar[...], bc[2])
        p0far[...] = nn(p1far, bc[2])

    for s in range(slots):
        inside = r + n_row * s >= c

        @pl.when(inside & (c == 1))
        def _():
            panel = nt(wcol[s], bc[2])
            panel = jnp.where(lower | (r + n_row * s > 1), panel, 0.0)
            o_ref[s] = jnp.where(listed[s] > 0, panel, 0.0)

        @pl.when(inside & (c >= 2))
        def _():
            product = nt(wcol[s], p0far[...])
            out = acc[s] - jnp.where(update[slots + s] > 0, product, 0.0)
            o_ref[s] = jnp.where(listed[s] > 0, out, 0.0)

        @pl.when(jnp.logical_not(inside))
        def _():
            o_ref[s] = jnp.zeros((width, width), jnp.float32)

    @pl.when(lead_a)
    def _():
        lead_copy(0).wait_send()

    @pl.when(lead_b)
    def _():
        lead_copy(1).wait_send()

    for s in range(slots):

        @pl.when(line_need(c + 2, s))
        def _():
            line_copy(s).wait_send()

        @pl.when(cross_need(cross, s))
        def _():
            cross_copy(s, x).wait_send()

    @pl.when((c >= 1) & (r == far_row))
    def _():
        for k in range(1, n_row):
            for q in range(2):
                far_copy(k, q).wait_send()

    for q in range(3):
        for h in range(2):
            for k in range(4):

                @pl.when(child[k][0])
                def _():
                    bc_copy(q, h, k).wait_send()


def on_device(n_row, n_col, matrix, present, update):
    tiles = matrix[:, 0, 0]
    slots, width = tiles.shape[0], tiles.shape[-1]
    tile = (width, width)
    dma = pltpu.SemaphoreType.DMA
    vmem = pl.BlockSpec(memory_space=pltpu.VMEM)
    smem = pl.BlockSpec(memory_space=pltpu.SMEM)
    out = pl.pallas_call(
        functools.partial(kernel, n_row, n_col),
        out_shape=jax.ShapeDtypeStruct(tiles.shape, jnp.float32),
        in_specs=[vmem, smem, smem],
        out_specs=vmem,
        scratch_shapes=[
            pltpu.VMEM((2, slots) + tile, jnp.float32),
            pltpu.VMEM((2,) + tile, jnp.float32),
            pltpu.VMEM((2,) + tile, jnp.float32),
            pltpu.VMEM((3,) + tile, jnp.float32),
            pltpu.VMEM((width, 2 * width), jnp.float32),
            pltpu.VMEM((slots,) + tile, jnp.float32),
            pltpu.VMEM((slots,) + tile, jnp.float32),
            pltpu.VMEM(tile, jnp.float32),
            pltpu.VMEM(tile, jnp.float32),
            dma((2, slots)),
            dma((2, slots)),
            dma((n_row, 2)),
            dma((2,)),
            dma((2,)),
            dma((2,)),
            dma((3, 2, 4)),
            dma((3, 2)),
        ],
        compiler_params=pltpu.CompilerParams(
            collective_id=0, has_side_effects=True, vmem_limit_bytes=40 * 1024 * 1024
        ),
    )(tiles, present.reshape(slots), update.reshape(2 * slots))
    return out[:, None, None]


def solution(mesh):
    return jax.shard_map(
        functools.partial(on_device, mesh.shape["row"], mesh.shape["col"]),
        mesh=mesh,
        in_specs=(
            P(None, "row", "col", None, None),
            P(None, "row", "col"),
            P(None, None, "row", "col"),
        ),
        out_specs=P(None, "row", "col", None, None),
        check_vma=False,
    )
```

profile of v0, /device:TPU:25, one launch (start us, length us, event | category | flops | bytes accessed | tf_op | source)
XLA Modules:
  0.0 68.2 jit_solution(15315696185153987979)
XLA Ops:
  0.0 0.0 copy-start.2
  0.0 0.5 broadcast.3
  0.5 0.2 copy-done.2
  0.7 0.7 reduce.3
  1.3 0.0 copy-start.1
  1.4 0.1 reshape.7.update
  1.4 0.6 copy-done.1
  2.0 0.0 copy-start
  2.0 1.2 %copy-done = f32[4,1,1,256,256]{4,3,2,1,0:T(8,128)S(1)} copy-done((f32[4,1,1,256,256]{4,3,2,1,0:T(8,128)S(1)}, f32[4,1,1,256,256]{4,3,2,1,0:T(8,128)}, u32[]{:S(2)}) %copy-start) | copy-done | bytes 1048600
  3.2 64.0 %shard_map.37 = f32[4,256,256]{2,1,0:T(8,128)S(1)} custom-call(f32[4,256,256]{2,1,0:T(8,128)S(1)} %bitcast.7, s32[4]{0:T(128)S(1)} %bitcast.8, s32[8]{0:T(128)S(1)} %reshape.7.update), custom_call_target="tpu_custom_call" | custom-call | tf_op jit(solution)/shard_map/pallas_call | solution.py:358
  67.3 1.0 %copy.6 = f32[4,1,1,256,256]{4,3,2,1,0:T(8,128)} copy(f32[4,1,1,256,256]{4,3,2,1,0:T(8,128)S(1)} %bitcast.6) | data formatting | bytes 2097152
Async XLA Ops:
  0.0 0.7 copy-start.2
  1.3 0.7 copy-start.1
  2.0 1.2 %copy-start = (f32[4,1,1,256,256]{4,3,2,1,0:T(8,128)S(1)}, f32[4,1,1,256,256]{4,3,2,1,0:T(8,128)}, u32[]{:S(2)}) copy-start(f32[4,1,1,256,256]{4,3,2,1,0:T(8,128)} %param.3) | copy-start | bytes 3145732
where the time goes:
time: 68.4 us; the launch traced here: 68.2 us
  Pallas kernels  64 us (94%)
  local copies, waits for them, and re-layouts  3.52 us (5%)
    pallas_call x1, Pallas kernels, on_device(): pl.pallas_call(functools.partial(kernel, n_row, n_col), out_shape=jax.Sha...  64 us
    unnamed x8, local copies, waits for them, and re-layouts  3.44 us

commit v1 on v0

v1 whole, which is shorter than its diff:
```python
import functools

import jax
import jax.numpy as jnp
from jax import lax
from jax.experimental import pallas as pl
from jax.experimental.pallas import tpu as pltpu
from jax.sharding import PartitionSpec as P

MESH = pl.DeviceIdType.MESH
HI = lax.Precision.HIGHEST
NB = 128
GROUP = 8
PIECES = 4


def dot(a, b, contract):
    return lax.dot_general(
        a, b, (contract, ((), ())), precision=HI, preferred_element_type=jnp.float32
    )


def nn(a, b):
    return dot(a, b, ((1,), (0,)))


def nt(a, b):
    return dot(a, b, ((1,), (1,)))


def tn(a, b):
    return dot(a, b, ((0,), (0,)))


def invert_block(m):
    n = m.shape[0]
    done = []
    for k in range(0, n, GROUP):
        cols = [jnp.broadcast_to(m[:, k + t : k + t + 1], m.shape) for t in range(GROUP)]
        rows = [m[t : t + 1, :] for t in range(GROUP)]
        total = None
        for t in range(GROUP):
            pivot = cols[t][t : t + 1, :]
            inverse = 1.0 / pivot
            done.append(rows[t] * lax.rsqrt(pivot))
            scaled = rows[t] * inverse
            for u in range(t + 1, GROUP):
                entry = cols[u][t : t + 1, :]
                rows[u] = rows[u] - entry * scaled
                cols[u] = cols[u] - cols[t] * (entry * inverse)
            term = cols[t] * scaled
            total = term if total is None else total + term
        m = m - total
        m = m[GROUP:]
    return jnp.concatenate(done, axis=0)


def inverse_factor(a, ready=None):
    n = a.shape[0]
    if n <= NB:
        eye = (
            lax.broadcasted_iota(jnp.int32, (n, n), 0)
            == lax.broadcasted_iota(jnp.int32, (n, n), 1)
        ).astype(jnp.float32)
        return invert_block(jnp.concatenate([a, eye], axis=1))[:, n:]
    h = n // 2
    first = inverse_factor(a[:h, :h])
    if ready is not None:
        ready(first)
    upper = nn(first, a[:h, h:])
    rest = a[h:, h:] - tn(upper, upper)
    below = tn(upper, first)
    last = inverse_factor(rest)
    return jnp.concatenate(
        [
            jnp.concatenate([first, jnp.zeros((h, h), jnp.float32)], axis=1),
            jnp.concatenate([-nn(last, below), last], axis=1),
        ],
        axis=0,
    )


def kernel(
    n_row, n_col, m_ref, listed, update, o_ref, dbuf, far, lead, bc, wcol, acc, wfar, p0far, p01,
    d_send, d_recv, far_send, far_recv, lead_send, lead_recv, bc_send, bc_recv,
):
    r = lax.axis_index("row")
    c = lax.axis_index("col")
    slots, width = m_ref.shape[0], m_ref.shape[-1]
    x = c % 2
    cross = c + 1 - 2 * x
    root = (r == 0) & (c == 0)
    lead_b = (r == 1) & (c == 1)
    far_row = c % n_row
    far_slot = jnp.minimum(c // n_row, slots - 1)

    def greet(row, col):
        pl.semaphore_signal(
            pltpu.get_barrier_semaphore(), inc=1, device_id=(row, col), device_id_type=MESH
        )

    barrier = pltpu.get_barrier_semaphore()
    for k in range(1, n_row):
        greet((r + k) % n_row, c)
    greet(r, cross)
    partners = n_row + (c >= 2).astype(jnp.int32) + (c + 2 < n_col).astype(jnp.int32)

    @pl.when(c >= 2)
    def _():
        greet(r, c - 2)

    @pl.when(c + 2 < n_col)
    def _():
        greet(r, c + 2)

    @pl.when(root)
    def _():
        greet(1, 1)

    @pl.when(lead_b)
    def _():
        greet(0, 0)

    @pl.when(c < 2)
    def _():
        dbuf[x] = m_ref[...]

    pl.semaphore_wait(barrier, partners + (root | lead_b).astype(jnp.int32))

    def lead_copy(q):
        return pltpu.make_async_remote_copy(
            m_ref.at[0], lead.at[q], lead_send.at[q], lead_recv.at[q],
            device_id=(0, 0), device_id_type=MESH,
        )

    lead_a = (r == 1) & (c == 0)

    @pl.when(lead_b)
    def _():
        lead_copy(1).start()

    part = width // PIECES

    def line_copy(s, h):
        piece = dbuf.at[x, s, pl.ds(h * part, part)]
        return pltpu.make_async_remote_copy(
            piece, piece, d_send.at[0, s, h], d_recv.at[0, s, h],
            device_id=(r, c + 2), device_id_type=MESH,
        )

    def cross_copy(s, h, side):
        piece = dbuf.at[side, s, pl.ds(h * part, part)]
        return pltpu.make_async_remote_copy(
            piece, piece, d_send.at[1, s, h], d_recv.at[1, s, h],
            device_id=(r, cross), device_id_type=MESH,
        )

    def line_need(col, s):
        return (col >= 2) & (col < n_col) & (r + n_row * s >= col - col % 2)

    def cross_need(col, s):
        return (col >= 1) & (r + n_row * s >= col)

    def travel(s):
        for h in range(PIECES):

            @pl.when(line_need(c, s))
            def _():
                line_copy(s, h).wait_recv()

            @pl.when(line_need(c + 2, s))
            def _():
                line_copy(s, h).start()

            @pl.when(cross_need(cross, s))
            def _():
                cross_copy(s, h, x).start()

    def arrive(s):
        @pl.when(cross_need(c, s))
        def _():
            for h in range(PIECES):
                cross_copy(s, h, 1 - x).wait_recv()

        @pl.when((c >= 1) & (r == far_row) & (far_slot == s))
        def _():
            for q in range(2):
                for k in range(n_row // 2):
                    far_copy(k, q, dbuf.at[q, s]).start()
                far[q] = dbuf[q, s]

    def far_copy(k, q, source):
        target = r + 1 - 2 * (r % 2) if k == 0 else (r + 2 * k) % n_row
        return pltpu.make_async_remote_copy(
            source, far.at[q], far_send.at[k, q], far_recv.at[q],
            device_id=(target, c), device_id_type=MESH,
        )

    half = width // 2
    quarter = width // 4
    triangle = [(0, half, half, 0), (half, quarter, width, 1), (half + quarter, quarter, width, 0)]
    full = [(h * quarter, quarter, width, h % 2) for h in range(4)]
    pieces = [triangle, full, triangle]
    start_row = [0, 1, 0]

    def child(q, line):
        p = start_row[q]
        mine = r % 2 == p
        over = c % 2 == line
        if line == 1:
            over = (over & jnp.logical_not((r == p) & (c == 1))) | ((r == p) & (c == 0))
        return [
            (mine & over, (r, cross)),
            (mine & (c % 2 == line) & (c + 2 < n_col), (r, c + 2)),
            (mine & (c == line) & (r + 2 < n_row), (r + 2, c)),
            (mine, (r + 1 - 2 * p, c)),
        ]

    def bc_copy(q, h, k):
        row, rows, cols, line = pieces[q][h]
        piece = bc.at[q, pl.ds(row, rows), pl.ds(0, cols)]
        return pltpu.make_async_remote_copy(
            piece, piece, bc_send.at[q, h, k], bc_recv.at[q, h],
            device_id=child(q, line)[k][1], device_id_type=MESH,
        )

    def bc_start(q, h):
        for k in range(4):

            @pl.when(child(q, pieces[q][h][3])[k][0])
            def _():
                bc_copy(q, h, k).start()

    def pass_on(q):
        @pl.when(jnp.logical_not((r == start_row[q]) & (c == 0)))
        def _():
            for h in range(len(pieces[q])):
                bc_copy(q, h, 0).wait_recv()
                bc_start(q, h)

    order = list(range(1, slots)) + [0]

    @pl.when(lead_a)
    def _():
        bc[1] = m_ref[0]
        for h in range(4):
            bc_start(1, h)

    @pl.when(jnp.logical_not(root))
    def _():
        for q in (0, 2):
            bc[q, :half, half:] = jnp.zeros((half, width - half), jnp.float32)

    travel(order[0])

    @pl.when(root)
    def _():
        for s in order[1:]:
            travel(s)

        def ready(q, first):
            bc[q, :half, :half] = first
            bc_start(q, 0)

        def rest(q, inverse):
            bc[q, :half, half:] = jnp.zeros((half, width - half), jnp.float32)
            bc[q, half:, :] = inverse[half:]
            bc_start(q, 1)
            bc_start(q, 2)

        first = inverse_factor(m_ref[0], functools.partial(ready, 0))
        rest(0, first)
        pass_on(1)
        lead_copy(1).wait_recv()
        cross01 = nt(bc[1], first)
        rest(2, inverse_factor(lead[1] - nt(cross01, cross01), functools.partial(ready, 2)))

    @pl.when(jnp.logical_not(root))
    def _():
        pass_on(1)
        arrive(order[0])
        for n, s in enumerate(order[1:]):
            travel(s)
            if n == len(order) - 2:
                pass_on(0)
            arrive(s)

    @pl.when((c >= 1) & (r != far_row))
    def _():
        for q in range(2):
            far_copy(0, q, far.at[q]).wait_recv()

            @pl.when(r % 2 == far_row % 2)
            def _():
                far_copy(0, q, far.at[q]).start()

    p01[...] = nt(bc[1], bc[0])

    lower = lax.broadcasted_iota(jnp.int32, (width, width), 0) >= lax.broadcasted_iota(
        jnp.int32, (width, width), 1
    )

    @pl.when(c >= 2)
    def _():
        p0far[...] = nt(far[0], bc[0])
        wfar[...] = far[1] - nt(p0far[...], p01[...])

    for s in range(slots):
        inside = r + n_row * s >= c

        @pl.when(inside & (c == 0))
        def _():
            panel = nt(m_ref[s], bc[0])
            panel = jnp.where(lower | (r + n_row * s > 0), panel, 0.0)
            o_ref[s] = jnp.where(listed[s] > 0, panel, 0.0)

        @pl.when(inside & (c >= 1))
        def _():
            panel = nt(dbuf[0, s], bc[0])
            wcol[s] = dbuf[1, s] - nt(panel, p01[...])

            @pl.when(c >= 2)
            def _():
                product = nt(panel, p0far[...])
                acc[s] = m_ref[s] - jnp.where(update[s] > 0, product, 0.0)

    @pl.when(jnp.logical_not(root))
    def _():
        pass_on(2)

    @pl.when(c >= 2)
    def _():
        p1far = nt(wfar[...], bc[2])
        p0far[...] = nn(p1far, bc[2])

    for s in range(slots):
        inside = r + n_row * s >= c

        @pl.when(inside & (c == 1))
        def _():
            panel = nt(wcol[s], bc[2])
            panel = jnp.where(lower | (r + n_row * s > 1), panel, 0.0)
            o_ref[s] = jnp.where(listed[s] > 0, panel, 0.0)

        @pl.when(inside & (c >= 2))
        def _():
            product = nt(wcol[s], p0far[...])
            out = acc[s] - jnp.where(update[slots + s] > 0, product, 0.0)
            o_ref[s] = jnp.where(listed[s] > 0, out, 0.0)

        @pl.when(jnp.logical_not(inside))
        def _():
            o_ref[s] = jnp.zeros((width, width), jnp.float32)

    @pl.when(lead_b)
    def _():
        lead_copy(1).wait_send()

    for s in range(slots):
        for h in range(PIECES):

            @pl.when(line_need(c + 2, s))
            def _():
                line_copy(s, h).wait_send()

            @pl.when(cross_need(cross, s))
            def _():
                cross_copy(s, h, x).wait_send()

    @pl.when((c >= 1) & (r == far_row))
    def _():
        for k in range(n_row // 2):
            for q in range(2):
                far_copy(k, q, dbuf.at[q, far_slot]).wait_send()

    @pl.when((c >= 1) & (r != far_row) & (r % 2 == far_row % 2))
    def _():
        for q in range(2):
            far_copy(0, q, far.at[q]).wait_send()

    for q in range(3):
        for h in range(len(pieces[q])):
            for k in range(4):

                @pl.when(child(q, pieces[q][h][3])[k][0])
                def _():
                    bc_copy(q, h, k).wait_send()


def on_device(n_row, n_col, matrix, present, update):
    tiles = matrix[:, 0, 0]
    slots, width = tiles.shape[0], tiles.shape[-1]
    tile = (width, width)
    dma = pltpu.SemaphoreType.DMA
    vmem = pl.BlockSpec(memory_space=pltpu.VMEM)
    smem = pl.BlockSpec(memory_space=pltpu.SMEM)
    out = pl.pallas_call(
        functools.partial(kernel, n_row, n_col),
        out_shape=jax.ShapeDtypeStruct(tiles.shape, jnp.float32),
        in_specs=[vmem, smem, smem],
        out_specs=vmem,
        scratch_shapes=[
            pltpu.VMEM((2, slots) + tile, jnp.float32),
            pltpu.VMEM((2,) + tile, jnp.float32),
            pltpu.VMEM((2,) + tile, jnp.float32),
            pltpu.VMEM((3,) + tile, jnp.float32),
            pltpu.VMEM((slots,) + tile, jnp.float32),
            pltpu.VMEM((slots,) + tile, jnp.float32),
            pltpu.VMEM(tile, jnp.float32),
            pltpu.VMEM(tile, jnp.float32),
            pltpu.VMEM(tile, jnp.float32),
            dma((2, slots, PIECES)),
            dma((2, slots, PIECES)),
            dma((n_row, 2)),
            dma((2,)),
            dma((2,)),
            dma((2,)),
            dma((3, 4, 4)),
            dma((3, 4)),
        ],
        compiler_params=pltpu.CompilerParams(
            collective_id=0, has_side_effects=True, vmem_limit_bytes=40 * 1024 * 1024
        ),
    )(tiles, present.reshape(slots), update.reshape(2 * slots))
    return out[:, None, None]


def solution(mesh):
    return jax.shard_map(
        functools.partial(on_device, mesh.shape["row"], mesh.shape["col"]),
        mesh=mesh,
        in_specs=(
            P(None, "row", "col", None, None),
            P(None, "row", "col"),
            P(None, None, "row", "col"),
        ),
        out_specs=P(None, "row", "col", None, None),
        check_vma=False,
    )
```

time: 68.4 us -> 82 us (1.20)
  the two profiles are of different devices: /device:TPU:25 before, /device:TPU:27 now
where the time goes in v1:
time: 82 us; the launch traced here: 81.8 us
  Pallas kernels  77.6 us (95%)
  local copies, waits for them, and re-layouts  3.52 us (4%)
    pallas_call x1, Pallas kernels, on_device(): pl.pallas_call(functools.partial(kernel, n_row, n_col), out_shape=jax.Sha...  77.6 us
    unnamed x8, local copies, waits for them, and re-layouts  3.44 us

profile of v1, /device:TPU:27, one launch (start us, length us, event | category | flops | bytes accessed | tf_op | source)
XLA Modules:
  0.0 81.8 jit_solution(1872329074908603105)
XLA Ops:
  0.0 0.0 copy-start.2
  0.0 0.5 broadcast.3
  0.5 0.2 copy-done.2
  0.7 0.7 reduce.3
  1.3 0.0 copy-start.1
  1.4 0.1 reshape.7.update
  1.4 0.6 copy-done.1
  2.0 0.0 copy-start
  2.0 1.2 %copy-done = f32[4,1,1,256,256]{4,3,2,1,0:T(8,128)S(1)} copy-done((f32[4,1,1,256,256]{4,3,2,1,0:T(8,128)S(1)}, f32[4,1,1,256,256]{4,3,2,1,0:T(8,128)}, u32[]{:S(2)}) %copy-start) | copy-done | bytes 1048600
  3.2 77.6 %shard_map.37 = f32[4,256,256]{2,1,0:T(8,128)S(1)} custom-call(f32[4,256,256]{2,1,0:T(8,128)S(1)} %bitcast.7, s32[4]{0:T(128)S(1)} %bitcast.8, s32[8]{0:T(128)S(1)} %reshape.7.update), custom_call_target="tpu_custom_call" | custom-call | tf_op jit(solution)/shard_map/pallas_call | solution.py:397
  80.9 1.0 %copy.6 = f32[4,1,1,256,256]{4,3,2,1,0:T(8,128)} copy(f32[4,1,1,256,256]{4,3,2,1,0:T(8,128)S(1)} %bitcast.6) | data formatting | bytes 2097152
Async XLA Ops:
  0.0 0.7 copy-start.2
  1.3 0.7 copy-start.1
  2.0 1.2 %copy-start = (f32[4,1,1,256,256]{4,3,2,1,0:T(8,128)S(1)}, f32[4,1,1,256,256]{4,3,2,1,0:T(8,128)}, u32[]{:S(2)}) copy-start(f32[4,1,1,256,256]{4,3,2,1,0:T(8,128)} %param.3) | copy-start | bytes 3145732

commit v2 on v0

--- a/solution.py
+++ b/solution.py
@@ -9,8 +9,8 @@
 
 MESH = pl.DeviceIdType.MESH
 HI = lax.Precision.HIGHEST
-NB = 64
-GROUP = 4
+NB = 128
+GROUP = 8
 
 
 def dot(a, b, contract):
@@ -35,56 +35,50 @@
     n = m.shape[0]
     done = []
     for k in range(0, n, GROUP):
-        top = (k // 8) * 8
-        off = k - top
         cols = [jnp.broadcast_to(m[:, k + t : k + t + 1], m.shape) for t in range(GROUP)]
-        rows = [m[off + t : off + t + 1, :] for t in range(GROUP)]
+        rows = [m[t : t + 1, :] for t in range(GROUP)]
         total = None
         for t in range(GROUP):
-            pivot = cols[t][off + t : off + t + 1, :]
+            pivot = cols[t][t : t + 1, :]
             inverse = 1.0 / pivot
             done.append(rows[t] * lax.rsqrt(pivot))
             scaled = rows[t] * inverse
             for u in range(t + 1, GROUP):
-                entry = cols[u][off + t : off + t + 1, :]
+                entry = cols[u][t : t + 1, :]
                 rows[u] = rows[u] - entry * scaled
                 cols[u] = cols[u] - cols[t] * (entry * inverse)
             term = cols[t] * scaled
             total = term if total is None else total + term
         m = m - total
-        if (k + GROUP) % 8 == 0:
-            m = m[8:]
+        m = m[GROUP:]
     return jnp.concatenate(done, axis=0)
 
 
-def inverse_factor(work, block_inv):
-    width = work.shape[0]
-    blocks = width // NB
-
-    def step(j, carry):
-        rows = pl.ds(pl.multiple_of(j * NB, NB), NB)
-        strip = work[rows, :]
-        diag = strip[:, :NB]
-        for b in range(1, blocks):
-            diag = jnp.where(j == b, strip[:, b * NB : (b + 1) * NB], diag)
+def inverse_factor(a):
+    n = a.shape[0]
+    if n <= NB:
         eye = (
-            lax.broadcasted_iota(jnp.int32, (NB, NB), 0)
-            == lax.broadcasted_iota(jnp.int32, (NB, NB), 1)
+            lax.broadcasted_iota(jnp.int32, (n, n), 0)
+            == lax.broadcasted_iota(jnp.int32, (n, n), 1)
         ).astype(jnp.float32)
-        solved = invert_block(jnp.concatenate([diag, eye], axis=1))
-        block = solved[:, NB:]
-        strip = nn(block, strip)
-        lane = lax.broadcasted_iota(jnp.int32, (NB, width), 1)
-        upper = jnp.where(lane >= (j + 1) * NB, strip[:, :width], 0.0)
-        work[...] = work[...] - tn(upper, strip)
-        work[rows, :] = strip
-        return carry
-
-    lax.fori_loop(0, blocks, step, 0)
+        return invert_block(jnp.concatenate([a, eye], axis=1))[:, n:]
+    h = n // 2
+    first = inverse_factor(a[:h, :h])
+    upper = nn(first, a[:h, h:])
+    rest = a[h:, h:] - tn(upper, upper)
+    below = tn(upper, first)
+    last = inverse_factor(rest)
+    return jnp.concatenate(
+        [
+            jnp.concatenate([first, jnp.zeros((h, h), jnp.float32)], axis=1),
+            jnp.concatenate([-nn(last, below), last], axis=1),
+        ],
+        axis=0,
+    )
 
 
 def kernel(
-    n_row, n_col, m_ref, listed, update, o_ref, dbuf, far, lead, bc, work, wcol, acc, wfar, p0far,
+    n_row, n_col, m_ref, listed, update, o_ref, dbuf, far, lead, bc, wcol, acc, wfar, p0far,
     d_send, d_recv, far_send, far_recv, lead_send, lead_recv, bc_send, bc_recv,
 ):
     r = lax.axis_index("row")
@@ -165,6 +159,25 @@
     def cross_need(col, s):
         return (col >= 1) & (r + n_row * s >= col)
 
+    def far_copy(k, q, source):
+        target = r + 1 - 2 * (r % 2) if k == 0 else (r + 2 * k) % n_row
+        return pltpu.make_async_remote_copy(
+            source, far.at[q], far_send.at[k, q], far_recv.at[q],
+            device_id=(target, c), device_id_type=MESH,
+        )
+
+    def arrive(s):
+        @pl.when(cross_need(c, s))
+        def _():
+            cross_copy(s, 1 - x).wait_recv()
+
+        @pl.when((c >= 1) & (r == far_row) & (far_slot == s))
+        def _():
+            for q in range(2):
+                for k in range(n_row // 2):
+                    far_copy(k, q, dbuf.at[q, s]).start()
+                far[q] = dbuf[q, s]
+
     for s in range(slots):
 
         @pl.when(line_need(c, s))
@@ -178,6 +191,8 @@
         @pl.when(cross_need(cross, s))
         def _():
             cross_copy(s, x).start()
+
+        arrive(s)
 
     child = [
         ((r % 2 == 0) & (c == 0) & (r + 2 < n_row), (r + 2, c)),
@@ -210,53 +225,28 @@
 
     @pl.when(root)
     def _():
-        eye = (
-            lax.broadcasted_iota(jnp.int32, (width, width), 0)
-            == lax.broadcasted_iota(jnp.int32, (width, width), 1)
-        ).astype(jnp.float32)
-        work[:, :width] = m_ref[0]
-        work[:, width:] = eye
-        inverse_factor(work, None)
-        bc[0] = work[:, width:]
+        first = inverse_factor(m_ref[0])
+        bc[0] = first
         bc_start(0, 0)
         bc_start(0, 1)
         lead_copy(0).wait_recv()
         lead_copy(1).wait_recv()
-        p01 = nt(lead[0], work[:, width:])
+        p01 = nt(lead[0], first)
         bc[1] = p01
         bc_start(1, 0)
         bc_start(1, 1)
-        work[:, :width] = lead[1] - nt(p01, p01)
-        work[:, width:] = eye
-        inverse_factor(work, None)
-        bc[2] = work[:, width:]
+        bc[2] = inverse_factor(lead[1] - nt(p01, p01))
         bc_start(2, 0)
         bc_start(2, 1)
 
-    for s in range(slots):
-
-        @pl.when(cross_need(c, s))
-        def _():
-            cross_copy(s, 1 - x).wait_recv()
-
-    def far_copy(k, q):
-        return pltpu.make_async_remote_copy(
-            dbuf.at[q, far_slot], far.at[q], far_send.at[k, q], far_recv.at[q],
-            device_id=((r + k) % n_row, c), device_id_type=MESH,
-        )
-
-    @pl.when((c >= 1) & (r == far_row))
-    def _():
-        for k in range(1, n_row):
-            for q in range(2):
-                far_copy(k, q).start()
+    @pl.when((c >= 1) & (r != far_row))
+    def _():
         for q in range(2):
-            far[q] = dbuf[q, far_slot]
-
-    @pl.when((c >= 1) & (r != far_row))
-    def _():
-        for q in range(2):
-            far_copy(1, q).wait_recv()
+            far_copy(0, q, far.at[q]).wait_recv()
+
+            @pl.when(r % 2 == far_row % 2)
+            def _():
+                far_copy(0, q, far.at[q]).start()
 
     pass_on(0)
     pass_on(1)
@@ -335,9 +325,14 @@
 
     @pl.when((c >= 1) & (r == far_row))
     def _():
-        for k in range(1, n_row):
+        for k in range(n_row // 2):
             for q in range(2):
-                far_copy(k, q).wait_send()
+                far_copy(k, q, dbuf.at[q, far_slot]).wait_send()
+
+    @pl.when((c >= 1) & (r != far_row) & (r % 2 == far_row % 2))
+    def _():
+        for q in range(2):
+            far_copy(0, q, far.at[q]).wait_send()
 
     for q in range(3):
         for h in range(2):
@@ -365,7 +360,6 @@
             pltpu.VMEM((2,) + tile, jnp.float32),
             pltpu.VMEM((2,) + tile, jnp.float32),
             pltpu.VMEM((3,) + tile, jnp.float32),
-            pltpu.VMEM((width, 2 * width), jnp.float32),
             pltpu.VMEM((slots,) + tile, jnp.float32),
             pltpu.VMEM((slots,) + tile, jnp.float32),
             pltpu.VMEM(tile, jnp.float32),

time: 68.4 us -> 64.7 us (0.946)
  the two profiles are of different devices: /device:TPU:25 before, /device:TPU:29 now
where the time goes in v2:
time: 64.7 us; the launch traced here: 64.5 us
  Pallas kernels  60.3 us (93%)
  local copies, waits for them, and re-layouts  3.52 us (5%)
  other arithmetic  0.66 us (1%)
    pallas_call x1, Pallas kernels, on_device(): pl.pallas_call(functools.partial(kernel, n_row, n_col), out_shape=jax.Sha...  60.3 us
    unnamed x8, local copies, waits for them, and re-layouts  3.44 us

profile of v2, /device:TPU:29, one launch (start us, length us, event | category | flops | bytes accessed | tf_op | source)
XLA Modules:
  0.0 64.5 jit_solution(8759274639803826340)
XLA Ops:
  0.0 0.0 copy-start.2
  0.0 0.5 broadcast.3
  0.5 0.2 copy-done.2
  0.7 0.7 %reduce.3 = s32[2,4]{1,0:T(2,128)S(1)} reduce(s32[2,4,1,1]{1,3,2,0:T(1,128)S(1)} %copy-done.2, s32[]{:T(128)} %broadcast.3), dimensions={2,3}, to_apply=%param.5.reduce_sub_computation.3 | reduce | bytes 68 | tf_op args[2]
  1.3 0.0 copy-start.1
  1.4 0.1 reshape.7.update
  1.4 0.6 copy-done.1
  2.0 0.0 copy-start
  2.0 1.2 %copy-done = f32[4,1,1,256,256]{4,3,2,1,0:T(8,128)S(1)} copy-done((f32[4,1,1,256,256]{4,3,2,1,0:T(8,128)S(1)}, f32[4,1,1,256,256]{4,3,2,1,0:T(8,128)}, u32[]{:S(2)}) %copy-start) | copy-done | bytes 1048600
  3.2 60.3 %shard_map.37 = f32[4,256,256]{2,1,0:T(8,128)S(1)} custom-call(f32[4,256,256]{2,1,0:T(8,128)S(1)} %bitcast.7, s32[4]{0:T(128)S(1)} %bitcast.8, s32[8]{0:T(128)S(1)} %reshape.7.update), custom_call_target="tpu_custom_call" | custom-call | tf_op jit(solution)/shard_map/pallas_call | solution.py:353
  63.5 1.0 %copy.6 = f32[4,1,1,256,256]{4,3,2,1,0:T(8,128)} copy(f32[4,1,1,256,256]{4,3,2,1,0:T(8,128)S(1)} %bitcast.6) | data formatting | bytes 2097152
Async XLA Ops:
  0.0 0.7 %copy-start.2 = (s32[2,4,1,1]{1,3,2,0:T(1,128)S(1)}, s32[2,4,1,1]{1,3,2,0:T(1,128)}, u32[]{:S(2)}) copy-start(s32[2,4,1,1]{1,3,2,0:T(1,128)} %param.5) | copy-start | bytes 100
  1.3 0.7 %copy-start.1 = (s32[4,1,1]{0,2,1:T(1,128)S(1)}, s32[4,1,1]{0,2,1:T(1,128)}, u32[]{:S(2)}) copy-start(s32[4,1,1]{0,2,1:T(1,128)} %param.4) | copy-start | bytes 52
  2.0 1.2 %copy-start = (f32[4,1,1,256,256]{4,3,2,1,0:T(8,128)S(1)}, f32[4,1,1,256,256]{4,3,2,1,0:T(8,128)}, u32[]{:S(2)}) copy-start(f32[4,1,1,256,256]{4,3,2,1,0:T(8,128)} %param.3) | copy-start | bytes 3145732
